TPU v7x, 128 devices: a whole 4x4x4 slice. The times are simulated.
128 devices in a mesh: segment: 8 (over y_lo, z), dp: 16 (over y_hi, x, core).
Axes of the slice: x: 4, y: 4 (y_hi: 2, y_lo: 2; y = y_hi * 2 + y_lo), z: 4, core: 2. Of those that a mesh axis runs over, the one named last changes fastest.
Arguments:
- tokens: bfloat16 [4, 512, 6144], P(None, 'dp'), may hold values from -18 to 18
- norm_gain: bfloat16 [6144], replicated, may hold values from 0.099609375 to 1.8984375
- router_weight: bfloat16 [6144, 8], replicated, may hold values from -0.078125 to 0.078125
- expert_ids: int32 [4, 512, 2], P(None, 'dp'), may hold values from 0 to 7, all different within a row; in each aligned block of 32 rows (0 to 31, 32 to 63, ..., all dimensions but the last counted through in order) at most 12 rows name the same one
- w_gate: bfloat16 [8, 6144, 8192], P('segment', None, 'dp'), may hold values from -0.078125 to 0.078125
- w_up: bfloat16 [8, 6144, 8192], P('segment', None, 'dp'), may hold values from -0.078125 to 0.078125
- w_down: bfloat16 [8, 8192, 6144], P('segment', 'dp'), may hold values from -0.0625 to 0.0625
Outputs:
- scored: bfloat16 [4, 512, 6144], P(None, 'dp', 'segment')
Inputs may be any that keep to these rules, and one draw needn't show every extreme that they name: `expert_ids`: each token names two different experts. In each micro-batch the 32 rows of one device name each expert at most 12 times, and in every draw some expert is named exactly 12 times by some device's rows.
All inputs are finite; a program needn't handle non-finite values.
Results may differ from a plain program's by a relative error of at most 0.0035.
Values may be sent and summed in bfloat16 or wider, within the bound.
A program may use at most 128 MiB of HBM per device.

v0:
```python
import jax
import jax.numpy as jnp
from jax import lax
from jax.sharding import PartitionSpec as P

epsilon = 1e-05


def rms_normed(tokens, norm_gain):
    widened = tokens.astype(jnp.float32)
    inverse_rms = lax.rsqrt(jnp.mean(widened * widened, axis=-1, keepdims=True) + epsilon)
    return (widened, (widened * inverse_rms * norm_gain.astype(jnp.float32)).astype(jnp.bfloat16))


def pair_gates(pair_ids, logits):
    expert_range = jnp.arange(logits.shape[-1], dtype=jnp.int32)
    first_logit = jnp.sum(jnp.where(pair_ids[..., 0:1] == expert_range, logits, 0.0), axis=-1)
    second_logit = jnp.sum(jnp.where(pair_ids[..., 1:2] == expert_range, logits, 0.0), axis=-1)
    return (jax.nn.sigmoid(first_logit - second_logit), jax.nn.sigmoid(second_logit - first_logit))


def expert_weight(pair_ids, first_gate, second_gate, expert):
    return jnp.where(pair_ids[..., 0] == expert, first_gate, 0.0) + jnp.where(
        pair_ids[..., 1] == expert, second_gate, 0.0
    )


def slot_table(pair_ids, expert, slot_count):
    chosen = jnp.any(pair_ids == expert, axis=-1)
    hit_count = chosen.astype(jnp.int32)
    position = jnp.cumsum(hit_count, axis=-1) - hit_count
    slot_range = jnp.arange(slot_count, dtype=jnp.int32)
    dispatch = chosen[..., None, :] & (position[..., None, :] == slot_range[:, None])
    return (position, dispatch)


def per_device(tokens, norm_gain, router_weight, expert_ids, w_gate, w_up, w_down):
    micro_count, tok_rows, model_width = tokens.shape
    expert_count = router_weight.shape[1]
    slot_count = 2 * tok_rows // expert_count + tok_rows // 8
    segment_count = lax.axis_size("segment")
    segment_index = lax.axis_index("segment")
    slice_width = model_width // segment_count
    gate_matrix = w_gate[0]
    up_matrix = w_up[0]
    down_matrix = w_down[0]
    widened, normed = rms_normed(tokens, norm_gain)
    logits = jnp.dot(
        normed.reshape(-1, model_width), router_weight, preferred_element_type=jnp.float32
    )
    logits = logits.reshape(micro_count, tok_rows, expert_count)
    first_gate, second_gate = pair_gates(expert_ids, logits)
    outputs = []
    positions = []
    for micro_index in range(micro_count):
        position, dispatch = slot_table(expert_ids[micro_index], segment_index, slot_count)
        routed = jnp.dot(
            dispatch.astype(jnp.bfloat16), normed[micro_index], preferred_element_type=jnp.float32
        ).astype(jnp.bfloat16)
        piece_rows = lax.all_gather(routed, "dp", axis=0, tiled=True)
        gate_proj = jnp.dot(piece_rows, gate_matrix, preferred_element_type=jnp.float32)
        up_proj = jnp.dot(piece_rows, up_matrix, preferred_element_type=jnp.float32)
        hidden = (jax.nn.silu(gate_proj) * up_proj).astype(jnp.bfloat16)
        outputs.append(
            lax.psum_scatter(
                jnp.dot(hidden, down_matrix, preferred_element_type=jnp.float32),
                "dp",
                scatter_dimension=0,
                tiled=True,
            )
        )
        positions.append(position)
    own_part = lax.dynamic_slice_in_dim(widened, segment_index * slice_width, slice_width, 2)
    placed = []
    for micro_index in range(micro_count):
        weight = expert_weight(
            expert_ids[micro_index],
            first_gate[micro_index],
            second_gate[micro_index],
            segment_index,
        )
        taken = jnp.take(
            outputs[micro_index], jnp.clip(positions[micro_index], 0, slot_count - 1), axis=0
        )
        placed.append(weight[:, None] * taken)
    summed = lax.psum_scatter(jnp.stack(placed), "segment", scatter_dimension=2, tiled=True)
    return (own_part + summed).astype(jnp.bfloat16)


def solution(mesh):
    placed = (
        P(None, "dp", None),
        P(),
        P(),
        P(None, "dp", None),
        P("segment", None, "dp"),
        P("segment", None, "dp"),
        P("segment", "dp", None),
    )
    return jax.shard_map(
        per_device, mesh=mesh, in_specs=placed, out_specs=P(None, "dp", "segment"), check_vma=False
    )
```

profile of v0, /device:TPU:0, one launch (start us, length us, event | category | flops | bytes accessed | tf_op | source)
XLA Modules:
  0.0 637.2 jit_solution(11767465393413596786)
XLA Ops:
  17.9 50.2 %all-gather.13.cloned.1.call-done = bf16[16,12,6144]{2,1,0:T(8,128)(2,1)} async-done(((bf16[1,12,6144]{2,1,0:T(8,128)(2,1)}), bf16[16,12,6144]{2,1,0:T(8,128)(2,1)}) %all-gather.13.cloned.1.call-update) | async-done | bytes 2359312 | tf_op jit(solution)/shard_map/all_gather | solution.py:60
  70.9 50.7 %all-gather.9.cloned.1.call-done = bf16[16,12,6144]{2,1,0:T(8,128)(2,1)} async-done(((bf16[1,12,6144]{2,1,0:T(8,128)(2,1)}), bf16[16,12,6144]{2,1,0:T(8,128)(2,1)}) %all-gather.9.cloned.1.call-update) | async-done | bytes 2359312 | tf_op jit(solution)/shard_map/all_gather | solution.py:60
  125.9 49.3 %all-gather.11.cloned.1.call-done = bf16[16,12,6144]{2,1,0:T(8,128)(2,1)} async-done(((bf16[1,12,6144]{2,1,0:T(8,128)(2,1)}), bf16[16,12,6144]{2,1,0:T(8,128)(2,1)}) %all-gather.11.cloned.1.call-update) | async-done | bytes 2359312 | tf_op jit(solution)/shard_map/all_gather | solution.py:60
  175.2 4.3 reshape.193
  179.4 5.0 fusion.28
  184.5 4.5 fusion.30
  191.1 37.4 %all-gather.15.cloned.1.call-done = bf16[16,12,6144]{2,1,0:T(8,128)(2,1)} async-done(((bf16[1,12,6144]{2,1,0:T(8,128)(2,1)}), bf16[16,12,6144]{2,1,0:T(8,128)(2,1)}) %all-gather.15.cloned.1.call-update) | async-done | bytes 2359312 | tf_op jit(solution)/shard_map/all_gather | solution.py:60
  232.8 5.7 fusion.24
  238.5 10.2 %fusion.8 = f32[192,6144]{1,0:T(8,128)} fusion(bf16[1,512,6144]{2,1,0:T(8,128)(2,1)} %param.15, bf16[192,6144]{1,0:T(8,128)(2,1)} %reshape.197, bf16[1,6144,512]{2,1,0:T(8,128)(2,1)} %param.14, f32[192,512]{1,0:T(8,128)} %fusion.24), kind=kOutput, calls=%fused_computation.12 | convolution fusion | flops 2416508928 | bytes 20054016 | tf_op jit(solution)/shard_map/dot_general | solution.py:66
  248.7 9.6 %fusion.10 = f32[192,6144]{1,0:T(8,128)} fusion(bf16[1,512,6144]{2,1,0:T(8,128)(2,1)} %param.15, bf16[192,6144]{1,0:T(8,128)(2,1)S(1)} %reshape.195, bf16[1,6144,512]{2,1,0:T(8,128)(2,1)} %param.14, f32[192,512]{1,0:T(8,128)} %fusion.26), kind=kOutput, calls=%fused_computation.14 | convolution fusion | flops 2416508928 | bytes 20054016 | tf_op jit(solution)/shard_map/dot_general | solution.py:66
  258.3 10.4 %fusion.14 = f32[192,6144]{1,0:T(8,128)} fusion(bf16[1,512,6144]{2,1,0:T(8,128)(2,1)} %param.15, bf16[192,6144]{1,0:T(8,128)(2,1)} %reshape.191, bf16[1,6144,512]{2,1,0:T(8,128)(2,1)} %param.14, f32[192,512]{1,0:T(8,128)S(1)} %fusion.30), kind=kOutput, calls=%fused_computation.18 | convolution fusion | flops 2416508928 | bytes 20054016 | tf_op jit(solution)/shard_map/dot_general | solution.py:66
  268.7 9.5 %fusion.12 = f32[192,6144]{1,0:T(8,128)} fusion(bf16[1,512,6144]{2,1,0:T(8,128)(2,1)} %param.15, bf16[192,6144]{1,0:T(8,128)(2,1)S(1)} %copy-done.4, bf16[1,6144,512]{2,1,0:T(8,128)(2,1)} %param.14, f32[192,512]{1,0:T(8,128)S(1)} %fusion.28), kind=kOutput, calls=%fused_computation.16 | convolution fusion | flops 2416508928 | bytes 20054016 | tf_op jit(solution)/shard_map/dot_general | solution.py:66
  278.2 145.2 %fusion.122 = (f32[16,6144]{1,0:T(8,128)S(1)}, f32[16,6144]{1,0:T(8,128)S(1)}, f32[16,6144]{1,0:T(8,128)S(1)}, f32[16,6144]{1,0:T(8,128)S(1)}) fusion(f32[192,6144]{1,0:T(8,128)} %fusion.8, f32[192,6144]{1,0:T(8,128)} %fusion.10, f32[192,6144]{1,0:T(8,128)} %fusion.12, f32[192,6144]{1,0:T(8,128)} %fusion.14), kind=kCustom, calls=%all-reduce-scatter.4 | all-reduce-scatter fusion | flops 6291457 | bytes 20447744
  430.3 5.2 collective-permute-start.15
  438.2 12.9 %collective-permute-done.15 = f32[12,6144]{1,0:T(8,128)S(1)} collective-permute-done((f32[12,6144]{1,0:T(8,128)S(1)}, f32[12,6144]{1,0:T(8,128)S(1)}, u32[]{:S(2)}, u32[]{:S(2)}) %collective-permute-start.15) | collective-permute-done | bytes 294944
  453.2 6.9 %collective-permute-start.8 = (f32[16,6144]{1,0:T(8,128)S(1)}, f32[16,6144]{1,0:T(8,128)}, u32[]{:S(2)}, u32[]{:S(2)}) collective-permute-start(f32[16,6144]{1,0:T(8,128)S(1)} %get-tuple-element.17), channel_id=1, source_target_pairs={{0,1},{1,2},{2,3},{3,4},{4,5},{5,6},{6,7},{7,8},{8,9},{9,10},{10,1... | collective-permute-start | bytes 1179656
  460.1 4.8 collective-permute-start.6
  465.0 8.2 %collective-permute-start.11 = (f32[12,6144]{1,0:T(8,128)S(1)}, f32[12,6144]{1,0:T(8,128)}, u32[]{:S(2)}, u32[]{:S(2)}) collective-permute-start(f32[12,6144]{1,0:T(8,128)S(1)} %slice.122), channel_id=1, source_target_pairs={{0,4},{1,5},{2,6},{3,7},{4,8},{5,9},{6,10},{7,11},{8,12},{9,13},{1... | collective-permute-start | bytes 884744
  473.2 18.5 %concatenate.3 = f32[76,6144]{1,0:T(8,128)} concatenate(f32[12,6144]{1,0:T(8,128)} %copy-done.5, f32[16,6144]{1,0:T(8,128)S(1)} %collective-permute-done.14, f32[16,6144]{1,0:T(8,128)} %collective-permute-done.13, f32[16,6144]{1,0:T(8,128)} %collective-permute-done.12, f32[16,6144]{1,0:T(8,128)S(1)} %get-tuple-element.16), dimensions={0} | concatenate | bytes 3735552
  500.1 6.9 %collective-permute-start.7 = (f32[12,6144]{1,0:T(8,128)S(1)}, f32[12,6144]{1,0:T(8,128)}, u32[]{:S(2)}, u32[]{:S(2)}) collective-permute-start(f32[12,6144]{1,0:T(8,128)S(1)} %slice.121), channel_id=1, source_target_pairs={{0,4},{1,5},{2,6},{3,7},{4,8},{5,9},{6,10},{7,11},{8,12},{9,13},{1... | collective-permute-start | bytes 884744
  507.0 18.8 %concatenate.2 = f32[76,6144]{1,0:T(8,128)} concatenate(f32[12,6144]{1,0:T(8,128)} %collective-permute-done.11, f32[16,6144]{1,0:T(8,128)} %collective-permute-done.10, f32[16,6144]{1,0:T(8,128)} %collective-permute-done.9, f32[16,6144]{1,0:T(8,128)} %collective-permute-done.8, f32[16,6144]{1,0:T(8,128)S(1)} %get-tuple-element.17), dimensions={0} | concatenate | bytes 3735552
  534.3 18.5 %concatenate.1 = f32[76,6144]{1,0:T(8,128)} concatenate(f32[12,6144]{1,0:T(8,128)} %collective-permute-done.7, f32[16,6144]{1,0:T(8,128)} %collective-permute-done.6, f32[16,6144]{1,0:T(8,128)S(1)} %collective-permute-done.5, f32[16,6144]{1,0:T(8,128)} %collective-permute-done.4, f32[16,6144]{1,0:T(8,128)S(1)} %get-tuple-element.18), dimensions={0} | concatenate | bytes 3735552
  554.0 18.3 %concatenate = f32[76,6144]{1,0:T(8,128)} concatenate(f32[12,6144]{1,0:T(8,128)} %collective-permute-done.3, f32[16,6144]{1,0:T(8,128)S(1)} %collective-permute-done.2, f32[16,6144]{1,0:T(8,128)S(1)} %collective-permute-done.1, f32[16,6144]{1,0:T(8,128)} %collective-permute-done, f32[16,6144]{1,0:T(8,128)S(1)} %get-tuple-element.19), dimensions={0} | concatenate | bytes 3735552
  584.4 44.4 %reduce-scatter.10.cloned.1.call-done = f32[4,32,768]{2,1,0:T(8,128)} async-done(((f32[4,32,6144]{2,1,0:T(8,128)}), f32[4,32,768]{2,1,0:T(8,128)}) %reduce-scatter.10.cloned.1.call-update) | async-done | bytes 393232 | tf_op jit(solution)/shard_map/reduce_scatter | solution.py:86
  (117 shorter events, 67.5 us)
Async XLA Ops:
  6.5 61.5 %all-gather.13.cloned.1.call-start = ((), (), s32[]{:S(2)}) async-start(), calls=%async_computation.4 | async-start | bytes 3342336 | tf_op jit(solution)/shard_map/all_gather | solution.py:60
  13.2 108.4 %all-gather.9.cloned.1.call-start = ((), (), s32[]{:S(2)}) async-start(), calls=%async_computation.2 | async-start | bytes 3342336 | tf_op jit(solution)/shard_map/all_gather | solution.py:60
  14.7 160.4 %all-gather.11.cloned.1.call-start = ((), (), s32[]{:S(2)}) async-start(), calls=%async_computation.3 | async-start | bytes 3342336 | tf_op jit(solution)/shard_map/all_gather | solution.py:60
  15.7 212.9 %all-gather.15.cloned.1.call-start = ((), (), s32[]{:S(2)}) async-start(), calls=%async_computation.5 | async-start | bytes 3342336 | tf_op jit(solution)/shard_map/all_gather | solution.py:60
  16.6 612.3 %reduce-scatter.10.cloned.1.call-start = ((), (), s32[]{:S(2)}) async-start(), calls=%async_computation.1 | async-start | bytes 3538944 | tf_op jit(solution)/shard_map/reduce_scatter | solution.py:86
  278.2 150.8 %copy-start.7 = (u32[128]{0:T(128)S(1)}, u32[128]{0:T(128)}, u32[]{:S(2)}) copy-start(u32[128]{0:T(128)} %constant.51) | copy-start | bytes 1540
  423.4 29.8 %collective-permute-start.14 = (f32[16,6144]{1,0:T(8,128)S(1)}, f32[16,6144]{1,0:T(8,128)S(1)}, u32[]{:S(2)}, u32[]{:S(2)}) collective-permute-start(f32[16,6144]{1,0:T(8,128)S(1)} %get-tuple-element.16), channel_id=1, source_target_pairs={{0,3},{1,4},{2,5},{3,6},{4,7},{5,8},{6,9},{7,10},{8,11},{9,12},{10... | collective-permute-start | bytes 1179656
  424.7 35.4 %collective-permute-start.13 = (f32[16,6144]{1,0:T(8,128)S(1)}, f32[16,6144]{1,0:T(8,128)}, u32[]{:S(2)}, u32[]{:S(2)}) collective-permute-start(f32[16,6144]{1,0:T(8,128)S(1)} %get-tuple-element.16), channel_id=1, source_target_pairs={{0,2},{1,3},{2,4},{3,5},{4,6},{5,7},{6,8},{7,9},{8,10},{9,11},{10,... | collective-permute-start | bytes 1179656
  426.8 38.2 %collective-permute-start.12 = (f32[16,6144]{1,0:T(8,128)S(1)}, f32[16,6144]{1,0:T(8,128)}, u32[]{:S(2)}, u32[]{:S(2)}) collective-permute-start(f32[16,6144]{1,0:T(8,128)S(1)} %get-tuple-element.16), channel_id=1, source_target_pairs={{0,1},{1,2},{2,3},{3,4},{4,5},{5,6},{6,7},{7,8},{8,9},{9,10},{10,1... | collective-permute-start | bytes 1179656
  430.3 20.9 %collective-permute-start.15 = (f32[12,6144]{1,0:T(8,128)S(1)}, f32[12,6144]{1,0:T(8,128)S(1)}, u32[]{:S(2)}, u32[]{:S(2)}) collective-permute-start(f32[12,6144]{1,0:T(8,128)S(1)} %slice.123), channel_id=1, source_target_pairs={{0,4},{1,5},{2,6},{3,7},{4,8},{5,9},{6,10},{7,11},{8,12},{9,13},{1... | collective-permute-start | bytes 884744
  435.6 59.0 %collective-permute-start.10 = (f32[16,6144]{1,0:T(8,128)S(1)}, f32[16,6144]{1,0:T(8,128)}, u32[]{:S(2)}, u32[]{:S(2)}) collective-permute-start(f32[16,6144]{1,0:T(8,128)S(1)} %get-tuple-element.17), channel_id=1, source_target_pairs={{0,3},{1,4},{2,5},{3,6},{4,7},{5,8},{6,9},{7,10},{8,11},{9,12},{10... | collective-permute-start | bytes 1179656
  451.1 13.8 %copy-start.5 = (f32[12,6144]{1,0:T(8,128)}, f32[12,6144]{1,0:T(8,128)S(1)}, u32[]{:S(2)}) copy-start(f32[12,6144]{1,0:T(8,128)S(1)} %collective-permute-done.15) | copy-start | bytes 884740
  451.1 45.5 %collective-permute-start.9 = (f32[16,6144]{1,0:T(8,128)S(1)}, f32[16,6144]{1,0:T(8,128)}, u32[]{:S(2)}, u32[]{:S(2)}) collective-permute-start(f32[16,6144]{1,0:T(8,128)S(1)} %get-tuple-element.17), channel_id=1, source_target_pairs={{0,2},{1,3},{2,4},{3,5},{4,6},{5,7},{6,8},{7,9},{8,10},{9,11},{10,... | collective-permute-start | bytes 1179656
  453.2 46.9 %collective-permute-start.8 = (f32[16,6144]{1,0:T(8,128)S(1)}, f32[16,6144]{1,0:T(8,128)}, u32[]{:S(2)}, u32[]{:S(2)}) collective-permute-start(f32[16,6144]{1,0:T(8,128)S(1)} %get-tuple-element.17), channel_id=1, source_target_pairs={{0,1},{1,2},{2,3},{3,4},{4,5},{5,6},{6,7},{7,8},{8,9},{9,10},{10,1... | collective-permute-start | bytes 1179656
  460.1 68.5 %collective-permute-start.6 = (f32[16,6144]{1,0:T(8,128)S(1)}, f32[16,6144]{1,0:T(8,128)}, u32[]{:S(2)}, u32[]{:S(2)}) collective-permute-start(f32[16,6144]{1,0:T(8,128)S(1)} %get-tuple-element.18), channel_id=1, source_target_pairs={{0,3},{1,4},{2,5},{3,6},{4,7},{5,8},{6,9},{7,10},{8,11},{9,12},{10... | collective-permute-start | bytes 1179656
  465.0 27.9 %collective-permute-start.11 = (f32[12,6144]{1,0:T(8,128)S(1)}, f32[12,6144]{1,0:T(8,128)}, u32[]{:S(2)}, u32[]{:S(2)}) collective-permute-start(f32[12,6144]{1,0:T(8,128)S(1)} %slice.122), channel_id=1, source_target_pairs={{0,4},{1,5},{2,6},{3,7},{4,8},{5,9},{6,10},{7,11},{8,12},{9,13},{1... | collective-permute-start | bytes 884744
  492.8 38.1 %collective-permute-start.5 = (f32[16,6144]{1,0:T(8,128)S(1)}, f32[16,6144]{1,0:T(8,128)S(1)}, u32[]{:S(2)}, u32[]{:S(2)}) collective-permute-start(f32[16,6144]{1,0:T(8,128)S(1)} %get-tuple-element.18), channel_id=1, source_target_pairs={{0,2},{1,3},{2,4},{3,5},{4,6},{5,7},{6,8},{7,9},{8,10},{9,11},{10,... | collective-permute-start | bytes 1179656
  494.6 39.7 %collective-permute-start.4 = (f32[16,6144]{1,0:T(8,128)S(1)}, f32[16,6144]{1,0:T(8,128)}, u32[]{:S(2)}, u32[]{:S(2)}) collective-permute-start(f32[16,6144]{1,0:T(8,128)S(1)} %get-tuple-element.18), channel_id=1, source_target_pairs={{0,1},{1,2},{2,3},{3,4},{4,5},{5,6},{6,7},{7,8},{8,9},{9,10},{10,1... | collective-permute-start | bytes 1179656
  496.7 57.2 %collective-permute-start.2 = (f32[16,6144]{1,0:T(8,128)S(1)}, f32[16,6144]{1,0:T(8,128)S(1)}, u32[]{:S(2)}, u32[]{:S(2)}) collective-permute-start(f32[16,6144]{1,0:T(8,128)S(1)} %get-tuple-element.19), channel_id=1, source_target_pairs={{0,3},{1,4},{2,5},{3,6},{4,7},{5,8},{6,9},{7,10},{8,11},{9,12},{10... | collective-permute-start | bytes 1179656
  500.1 26.8 %collective-permute-start.7 = (f32[12,6144]{1,0:T(8,128)S(1)}, f32[12,6144]{1,0:T(8,128)}, u32[]{:S(2)}, u32[]{:S(2)}) collective-permute-start(f32[12,6144]{1,0:T(8,128)S(1)} %slice.121), channel_id=1, source_target_pairs={{0,4},{1,5},{2,6},{3,7},{4,8},{5,9},{6,10},{7,11},{8,12},{9,13},{1... | collective-permute-start | bytes 884744
  526.9 27.0 %collective-permute-start.1 = (f32[16,6144]{1,0:T(8,128)S(1)}, f32[16,6144]{1,0:T(8,128)S(1)}, u32[]{:S(2)}, u32[]{:S(2)}) collective-permute-start(f32[16,6144]{1,0:T(8,128)S(1)} %get-tuple-element.19), channel_id=1, source_target_pairs={{0,2},{1,3},{2,4},{3,5},{4,6},{5,7},{6,8},{7,9},{8,10},{9,11},{10,... | collective-permute-start | bytes 1179656
  528.6 25.3 %collective-permute-start = (f32[16,6144]{1,0:T(8,128)S(1)}, f32[16,6144]{1,0:T(8,128)}, u32[]{:S(2)}, u32[]{:S(2)}) collective-permute-start(f32[16,6144]{1,0:T(8,128)S(1)} %get-tuple-element.19), channel_id=1, source_target_pairs={{0,1},{1,2},{2,3},{3,4},{4,5},{5,6},{6,7},{7,8},{8,9},{9,10},{10,1... | collective-permute-start | bytes 1179656
  530.9 23.0 %collective-permute-start.3 = (f32[12,6144]{1,0:T(8,128)S(1)}, f32[12,6144]{1,0:T(8,128)}, u32[]{:S(2)}, u32[]{:S(2)}) collective-permute-start(f32[12,6144]{1,0:T(8,128)S(1)} %slice.120), channel_id=1, source_target_pairs={{0,4},{1,5},{2,6},{3,7},{4,8},{5,9},{6,10},{7,11},{8,12},{9,13},{1... | collective-permute-start | bytes 884744
  582.4 48.3 %copy-start.1 = (bf16[6144,8]{0,1:T(8,128)(2,1)S(1)}, bf16[6144,8]{0,1:T(8,128)(2,1)}, u32[]{:S(2)}) copy-start(bf16[6144,8]{0,1:T(8,128)(2,1)} %param.11) | copy-start | bytes 294916
  (7 other events, 47.3 us)
Sparse Core Ops, SparseCore 0:
  13.3 54.7 all-gather.12
  70.5 51.0 all-gather.8
  124.1 51.0 all-gather.10
  177.5 51.0 all-gather.14
  581.2 47.6 reduce-scatter.9
where the time goes:
time: 641 us; the launch traced here: 637 us
  waiting for transfers between devices  245 us (38%)
  blocking collectives  145 us (23%)
  local copies, waits for them, and re-layouts  101 us (16%)
  matrix products  61.6 us (10%)
  starting transfers between devices  57.1 us (9%)
  between operations  14.2 us (2%)
  other arithmetic  13.3 us (2%)
    all_gather x4, waiting for transfers between devices, per_device(): piece_rows = lax.all_gather(routed, 'dp', axis=0, tiled=True)  188 us
    unnamed x1, blocking collectives  145 us
    unnamed x37, local copies, waits for them, and re-layouts  96.3 us
    unnamed x16, starting transfers between devices  56.9 us
    reduce_scatter x1, waiting for transfers between devices, per_device(): lax.psum_scatter(jnp.stack(placed), 'segment', scatter_dimension=2, tiled...  44.4 us
    dot_general x4, matrix products, per_device(): jnp.dot(hidden, down_matrix, preferred_element_type=jnp.float32)  39.7 us
    dot_general x4, matrix products, per_device(): jnp.dot(piece_rows, gate_matrix, preferred_element_type=jnp.float32)  17.3 us
    unnamed x21, waiting for transfers between devices  13 us
  transfers between devices with their start and end apart: 21, of which 6 were waited for; matrix products, arithmetic and copies ran while one was open for 14% of the time, Pallas kernels for 0%

commit v1 on v0

--- a/solution.py
+++ b/solution.py
@@ -4,6 +4,13 @@
 from jax.sharding import PartitionSpec as P
 
 epsilon = 1e-05
+
+
+def exchange_gather(x, mesh_axis, along):
+    size = lax.axis_size(mesh_axis)
+    blocks = jnp.stack([x for _ in range(size)])
+    blocks = lax.all_to_all(blocks, mesh_axis, split_axis=0, concat_axis=0)
+    return jnp.concatenate(blocks, axis=along)
 
 
 def rms_normed(tokens, norm_gain):
@@ -57,7 +64,7 @@
         routed = jnp.dot(
             dispatch.astype(jnp.bfloat16), normed[micro_index], preferred_element_type=jnp.float32
         ).astype(jnp.bfloat16)
-        piece_rows = lax.all_gather(routed, "dp", axis=0, tiled=True)
+        piece_rows = exchange_gather(routed, "dp", 0)
         gate_proj = jnp.dot(piece_rows, gate_matrix, preferred_element_type=jnp.float32)
         up_proj = jnp.dot(piece_rows, up_matrix, preferred_element_type=jnp.float32)
         hidden = (jax.nn.silu(gate_proj) * up_proj).astype(jnp.bfloat16)

time: 641 us -> 598 us (0.933)
  waiting for transfers between devices: 245 us -> 164 us
  starting transfers between devices: 57.1 us -> 89.2 us
    all_gather x4 -> x0, waiting for transfers between devices: 188 us -> none  [per_device(): piece_rows = lax.all_gather(routed, 'dp', axis=0, tiled=True)]
    all_to_all x0 -> x4, waiting for transfers between devices: none -> 110 us  [exchange_gather(): blocks = lax.all_to_all(blocks, mesh_axis, split_axis=0, concat_axis=0)]
    all_to_all x0 -> x4, starting transfers between devices: none -> 25 us  [exchange_gather(): blocks = lax.all_to_all(blocks, mesh_axis, split_axis=0, concat_axis=0)]
    unnamed x37 -> x31, local copies, waits for them, and re-layouts: 96.3 us -> 80.7 us
    reshape x0 -> x4, local copies, waits for them, and re-layouts: none -> 13.6 us  [exchange_gather(): return jnp.concatenate(blocks, axis=along)]
    another operation x0 -> x4, local copies, waits for them, and re-layouts: none -> 8.13 us  [exchange_gather(): blocks = jnp.stack([x for _ in range(size)])]
    unnamed x16, starting transfers between devices: 56.9 us -> 64 us
    unnamed x21 -> x17, waiting for transfers between devices: 13 us -> 10.8 us
  transfers between devices with their start and end apart: 21 -> 21, of which waited for: 6 -> 6; matrix products, arithmetic and copies ran while one was open for 14% -> 20% of each run, Pallas kernels for 0% -> 0%
where the time goes in v1:
time: 598 us; the launch traced here: 594 us
  waiting for transfers between devices  164 us (27%)
  blocking collectives  145 us (24%)
  local copies, waits for them, and re-layouts  107 us (18%)
  starting transfers between devices  89.2 us (15%)
  matrix products  61.3 us (10%)
  between operations  14.5 us (2%)
  other arithmetic  13.3 us (2%)
    unnamed x1, blocking collectives  145 us
    all_to_all x4, waiting for transfers between devices, exchange_gather(): blocks = lax.all_to_all(blocks, mesh_axis, split_axis=0, concat_axis=0)  110 us
    unnamed x31, local copies, waits for them, and re-layouts  80.7 us
    unnamed x16, starting transfers between devices  64 us
    reduce_scatter x1, waiting for transfers between devices, per_device(): lax.psum_scatter(jnp.stack(placed), 'segment', scatter_dimension=2, tiled...  42.9 us
    dot_general x4, matrix products, per_device(): jnp.dot(hidden, down_matrix, preferred_element_type=jnp.float32)  39.5 us
    all_to_all x4, starting transfers between devices, exchange_gather(): blocks = lax.all_to_all(blocks, mesh_axis, split_axis=0, concat_axis=0)  25 us
    dot_general x4, matrix products, per_device(): jnp.dot(piece_rows, gate_matrix, preferred_element_type=jnp.float32)  19.9 us
  transfers between devices with their start and end apart: 21, of which 6 were waited for; matrix products, arithmetic and copies ran while one was open for 20% of the time, Pallas kernels for 0%

profile of v1, /device:TPU:0, one launch (start us, length us, event | category | flops | bytes accessed | tf_op | source)
XLA Modules:
  0.0 594.4 jit_solution(9140829957652679538)
XLA Ops:
  14.5 7.2 %all-to-all-start = ((bf16[16,12,6144]{2,1,0:T(8,128)(2,1)}), bf16[16,12,6144]{2,1,0:T(8,128)(2,1)}, u32[]{:S(2)}, u32[]{:S(2)}) async-start(bf16[16,12,6144]{2,1,0:T(8,128)(2,1)} %stack.18), calls=%async_computation | async-start | bytes 6291456 | tf_op jit(solution)/shard_map/all_to_all | solution.py:12
  21.9 42.2 %all-to-all-done = bf16[16,12,6144]{2,1,0:T(8,128)(2,1)} async-done(((bf16[16,12,6144]{2,1,0:T(8,128)(2,1)}), bf16[16,12,6144]{2,1,0:T(8,128)(2,1)}, u32[]{:S(2)}, u32[]{:S(2)}) %all-to-all-start) | async-done | bytes 2359328 | tf_op jit(solution)/shard_map/all_to_all | solution.py:12
  66.1 6.1 %all-to-all-start.1 = ((bf16[16,12,6144]{2,1,0:T(8,128)(2,1)}), bf16[16,12,6144]{2,1,0:T(8,128)(2,1)}, u32[]{:S(2)}, u32[]{:S(2)}) async-start(bf16[16,12,6144]{2,1,0:T(8,128)(2,1)} %stack.20), calls=%async_computation.1 | async-start | bytes 6291456 | tf_op jit(solution)/shard_map/all_to_all | solution.py:12
  74.4 40.2 %all-to-all-done.1 = bf16[16,12,6144]{2,1,0:T(8,128)(2,1)} async-done(((bf16[16,12,6144]{2,1,0:T(8,128)(2,1)}), bf16[16,12,6144]{2,1,0:T(8,128)(2,1)}, u32[]{:S(2)}, u32[]{:S(2)}) %all-to-all-start.1) | async-done | bytes 2359328 | tf_op jit(solution)/shard_map/all_to_all | solution.py:12
  116.6 5.9 all-to-all-start.2
  141.8 10.2 %fusion.10 = f32[192,6144]{1,0:T(8,128)} fusion(bf16[1,512,6144]{2,1,0:T(8,128)(2,1)} %param.15, bf16[192,6144]{1,0:T(8,128)(2,1)} %reshape.167, bf16[1,6144,512]{2,1,0:T(8,128)(2,1)} %param.14, f32[192,512]{1,0:T(8,128)} %fusion.26), kind=kOutput, calls=%fused_computation.14 | convolution fusion | flops 2416508928 | bytes 20054016 | tf_op jit(solution)/shard_map/dot_general | solution.py:73
  152.1 12.8 %all-to-all-done.2 = bf16[16,12,6144]{2,1,0:T(8,128)(2,1)S(1)} async-done(((bf16[16,12,6144]{2,1,0:T(8,128)(2,1)}), bf16[16,12,6144]{2,1,0:T(8,128)(2,1)S(1)}, u32[]{:S(2)}, u32[]{:S(2)}) %all-to-all-start.2) | async-done | bytes 2359328 | tf_op jit(solution)/shard_map/all_to_all | solution.py:12
  166.9 5.8 all-to-all-start.3
  180.2 9.6 %fusion.8 = f32[192,6144]{1,0:T(8,128)} fusion(bf16[1,512,6144]{2,1,0:T(8,128)(2,1)} %param.15, bf16[192,6144]{1,0:T(8,128)(2,1)S(1)} %copy-done.4, bf16[1,6144,512]{2,1,0:T(8,128)(2,1)} %param.14, f32[192,512]{1,0:T(8,128)S(1)} %copy-done.6), kind=kOutput, calls=%fused_computation.12 | convolution fusion | flops 2416508928 | bytes 20054016 | tf_op jit(solution)/shard_map/dot_general | solution.py:73
  189.8 10.2 %fusion.6 = f32[192,6144]{1,0:T(8,128)} fusion(bf16[1,512,6144]{2,1,0:T(8,128)(2,1)} %param.15, bf16[192,6144]{1,0:T(8,128)(2,1)} %reshape.171, bf16[1,6144,512]{2,1,0:T(8,128)(2,1)} %param.14, f32[192,512]{1,0:T(8,128)S(1)} %fusion.22), kind=kOutput, calls=%fused_computation.10 | convolution fusion | flops 2416508928 | bytes 20054016 | tf_op jit(solution)/shard_map/dot_general | solution.py:73
  200.0 15.1 %all-to-all-done.3 = bf16[16,12,6144]{2,1,0:T(8,128)(2,1)} async-done(((bf16[16,12,6144]{2,1,0:T(8,128)(2,1)}), bf16[16,12,6144]{2,1,0:T(8,128)(2,1)}, u32[]{:S(2)}, u32[]{:S(2)}) %all-to-all-start.3) | async-done | bytes 2359328 | tf_op jit(solution)/shard_map/all_to_all | solution.py:12
  222.1 9.5 %fusion.4 = f32[192,6144]{1,0:T(8,128)} fusion(bf16[1,512,6144]{2,1,0:T(8,128)(2,1)} %param.15, bf16[192,6144]{1,0:T(8,128)(2,1)S(1)} %reshape.173, bf16[1,6144,512]{2,1,0:T(8,128)(2,1)} %param.14, f32[192,512]{1,0:T(8,128)S(1)} %fusion.20), kind=kOutput, calls=%fused_computation.8 | convolution fusion | flops 2416508928 | bytes 20054016 | tf_op jit(solution)/shard_map/dot_general | solution.py:73
  231.6 145.2 %fusion.118 = (f32[16,6144]{1,0:T(8,128)S(1)}, f32[16,6144]{1,0:T(8,128)S(1)}, f32[16,6144]{1,0:T(8,128)S(1)}, f32[16,6144]{1,0:T(8,128)S(1)}) fusion(f32[192,6144]{1,0:T(8,128)} %fusion.4, f32[192,6144]{1,0:T(8,128)} %fusion.6, f32[192,6144]{1,0:T(8,128)} %fusion.8, f32[192,6144]{1,0:T(8,128)} %fusion.10), kind=kCustom, calls=%all-reduce-scatter.4 | all-reduce-scatter fusion | flops 6291457 | bytes 20447744
  384.0 7.0 %collective-permute-start.15 = (f32[12,6144]{1,0:T(8,128)S(1)}, f32[12,6144]{1,0:T(8,128)S(1)}, u32[]{:S(2)}, u32[]{:S(2)}) collective-permute-start(f32[12,6144]{1,0:T(8,128)S(1)} %slice.123), channel_id=1, source_target_pairs={{0,4},{1,5},{2,6},{3,7},{4,8},{5,9},{6,10},{7,11},{8,12},{9,13},{1... | collective-permute-start | bytes 884744
  393.7 10.7 %collective-permute-done.15 = f32[12,6144]{1,0:T(8,128)S(1)} collective-permute-done((f32[12,6144]{1,0:T(8,128)S(1)}, f32[12,6144]{1,0:T(8,128)S(1)}, u32[]{:S(2)}, u32[]{:S(2)}) %collective-permute-start.15) | collective-permute-done | bytes 294944
  406.5 9.7 %collective-permute-start.8 = (f32[16,6144]{1,0:T(8,128)S(1)}, f32[16,6144]{1,0:T(8,128)}, u32[]{:S(2)}, u32[]{:S(2)}) collective-permute-start(f32[16,6144]{1,0:T(8,128)S(1)} %get-tuple-element.17), channel_id=1, source_target_pairs={{0,1},{1,2},{2,3},{3,4},{4,5},{5,6},{6,7},{7,8},{8,9},{9,10},{10,1... | collective-permute-start | bytes 1179656
  416.2 5.9 collective-permute-start.6
  422.1 9.2 %collective-permute-start.11 = (f32[12,6144]{1,0:T(8,128)S(1)}, f32[12,6144]{1,0:T(8,128)}, u32[]{:S(2)}, u32[]{:S(2)}) collective-permute-start(f32[12,6144]{1,0:T(8,128)S(1)} %slice.122), channel_id=1, source_target_pairs={{0,4},{1,5},{2,6},{3,7},{4,8},{5,9},{6,10},{7,11},{8,12},{9,13},{1... | collective-permute-start | bytes 884744
  431.3 18.5 %concatenate.3 = f32[76,6144]{1,0:T(8,128)} concatenate(f32[12,6144]{1,0:T(8,128)} %copy-done.5, f32[16,6144]{1,0:T(8,128)S(1)} %collective-permute-done.14, f32[16,6144]{1,0:T(8,128)} %collective-permute-done.13, f32[16,6144]{1,0:T(8,128)} %collective-permute-done.12, f32[16,6144]{1,0:T(8,128)S(1)} %get-tuple-element.16), dimensions={0} | concatenate | bytes 3735552
  456.1 6.8 %collective-permute-start.7 = (f32[12,6144]{1,0:T(8,128)S(1)}, f32[12,6144]{1,0:T(8,128)}, u32[]{:S(2)}, u32[]{:S(2)}) collective-permute-start(f32[12,6144]{1,0:T(8,128)S(1)} %slice.121), channel_id=1, source_target_pairs={{0,4},{1,5},{2,6},{3,7},{4,8},{5,9},{6,10},{7,11},{8,12},{9,13},{1... | collective-permute-start | bytes 884744
  462.9 18.8 %concatenate.2 = f32[76,6144]{1,0:T(8,128)} concatenate(f32[12,6144]{1,0:T(8,128)} %collective-permute-done.11, f32[16,6144]{1,0:T(8,128)} %collective-permute-done.10, f32[16,6144]{1,0:T(8,128)} %collective-permute-done.9, f32[16,6144]{1,0:T(8,128)} %collective-permute-done.8, f32[16,6144]{1,0:T(8,128)S(1)} %get-tuple-element.17), dimensions={0} | concatenate | bytes 3735552
  492.6 18.5 %concatenate.1 = f32[76,6144]{1,0:T(8,128)} concatenate(f32[12,6144]{1,0:T(8,128)} %collective-permute-done.7, f32[16,6144]{1,0:T(8,128)} %collective-permute-done.6, f32[16,6144]{1,0:T(8,128)S(1)} %collective-permute-done.5, f32[16,6144]{1,0:T(8,128)} %collective-permute-done.4, f32[16,6144]{1,0:T(8,128)S(1)} %get-tuple-element.18), dimensions={0} | concatenate | bytes 3735552
  512.3 18.3 %concatenate = f32[76,6144]{1,0:T(8,128)} concatenate(f32[12,6144]{1,0:T(8,128)} %collective-permute-done.3, f32[16,6144]{1,0:T(8,128)S(1)} %collective-permute-done.2, f32[16,6144]{1,0:T(8,128)S(1)} %collective-permute-done.1, f32[16,6144]{1,0:T(8,128)} %collective-permute-done, f32[16,6144]{1,0:T(8,128)S(1)} %get-tuple-element.19), dimensions={0} | concatenate | bytes 3735552
  542.8 42.9 %reduce-scatter.10.cloned.1.call-done = f32[4,32,768]{2,1,0:T(8,128)} async-done(((f32[4,32,6144]{2,1,0:T(8,128)}), f32[4,32,768]{2,1,0:T(8,128)}) %reduce-scatter.10.cloned.1.call-update) | async-done | bytes 393232 | tf_op jit(solution)/shard_map/reduce_scatter | solution.py:93
  (114 shorter events, 93.5 us)
Async XLA Ops:
  6.5 66.2 %copy-start = (bf16[6144,8]{0,1:T(8,128)(2,1)S(1)}, bf16[6144,8]{0,1:T(8,128)(2,1)}, u32[]{:S(2)}) copy-start(bf16[6144,8]{0,1:T(8,128)(2,1)} %param.11) | copy-start | bytes 294916
  14.5 49.5 %all-to-all-start = ((bf16[16,12,6144]{2,1,0:T(8,128)(2,1)}), bf16[16,12,6144]{2,1,0:T(8,128)(2,1)}, u32[]{:S(2)}, u32[]{:S(2)}) async-start(bf16[16,12,6144]{2,1,0:T(8,128)(2,1)} %stack.18), calls=%async_computation | async-start | bytes 6291456 | tf_op jit(solution)/shard_map/all_to_all | solution.py:12
  66.1 48.4 %all-to-all-start.1 = ((bf16[16,12,6144]{2,1,0:T(8,128)(2,1)}), bf16[16,12,6144]{2,1,0:T(8,128)(2,1)}, u32[]{:S(2)}, u32[]{:S(2)}) async-start(bf16[16,12,6144]{2,1,0:T(8,128)(2,1)} %stack.20), calls=%async_computation.1 | async-start | bytes 6291456 | tf_op jit(solution)/shard_map/all_to_all | solution.py:12
  116.6 48.3 %all-to-all-start.2 = ((bf16[16,12,6144]{2,1,0:T(8,128)(2,1)}), bf16[16,12,6144]{2,1,0:T(8,128)(2,1)S(1)}, u32[]{:S(2)}, u32[]{:S(2)}) async-start(bf16[16,12,6144]{2,1,0:T(8,128)(2,1)} %stack.22), calls=%async_computation.2 | async-start | bytes 6291456 | tf_op jit(solution)/shard_map/all_to_all | solution.py:12
  166.9 48.2 %all-to-all-start.3 = ((bf16[16,12,6144]{2,1,0:T(8,128)(2,1)}), bf16[16,12,6144]{2,1,0:T(8,128)(2,1)}, u32[]{:S(2)}, u32[]{:S(2)}) async-start(bf16[16,12,6144]{2,1,0:T(8,128)(2,1)} %stack.24), calls=%async_computation.3 | async-start | bytes 6291456 | tf_op jit(solution)/shard_map/all_to_all | solution.py:12
  172.7 413.0 %reduce-scatter.10.cloned.1.call-start = ((), (), s32[]{:S(2)}) async-start(), calls=%async_computation.5 | async-start | bytes 3538944 | tf_op jit(solution)/shard_map/reduce_scatter | solution.py:93
  231.6 151.1 %copy-start.8 = (u32[128]{0:T(128)S(1)}, u32[128]{0:T(128)}, u32[]{:S(2)}) copy-start(u32[128]{0:T(128)} %constant.51) | copy-start | bytes 1540
  376.8 29.7 %collective-permute-start.14 = (f32[16,6144]{1,0:T(8,128)S(1)}, f32[16,6144]{1,0:T(8,128)S(1)}, u32[]{:S(2)}, u32[]{:S(2)}) collective-permute-start(f32[16,6144]{1,0:T(8,128)S(1)} %get-tuple-element.16), channel_id=1, source_target_pairs={{0,3},{1,4},{2,5},{3,6},{4,7},{5,8},{6,9},{7,10},{8,11},{9,12},{10... | collective-permute-start | bytes 1179656
  378.1 38.1 %collective-permute-start.13 = (f32[16,6144]{1,0:T(8,128)S(1)}, f32[16,6144]{1,0:T(8,128)}, u32[]{:S(2)}, u32[]{:S(2)}) collective-permute-start(f32[16,6144]{1,0:T(8,128)S(1)} %get-tuple-element.16), channel_id=1, source_target_pairs={{0,2},{1,3},{2,4},{3,5},{4,6},{5,7},{6,8},{7,9},{8,10},{9,11},{10,... | collective-permute-start | bytes 1179656
  380.2 41.9 %collective-permute-start.12 = (f32[16,6144]{1,0:T(8,128)S(1)}, f32[16,6144]{1,0:T(8,128)}, u32[]{:S(2)}, u32[]{:S(2)}) collective-permute-start(f32[16,6144]{1,0:T(8,128)S(1)} %get-tuple-element.16), channel_id=1, source_target_pairs={{0,1},{1,2},{2,3},{3,4},{4,5},{5,6},{6,7},{7,8},{8,9},{9,10},{10,1... | collective-permute-start | bytes 1179656
  384.0 20.5 %collective-permute-start.15 = (f32[12,6144]{1,0:T(8,128)S(1)}, f32[12,6144]{1,0:T(8,128)S(1)}, u32[]{:S(2)}, u32[]{:S(2)}) collective-permute-start(f32[12,6144]{1,0:T(8,128)S(1)} %slice.123), channel_id=1, source_target_pairs={{0,4},{1,5},{2,6},{3,7},{4,8},{5,9},{6,10},{7,11},{8,12},{9,13},{1... | collective-permute-start | bytes 884744
  391.1 61.6 %collective-permute-start.10 = (f32[16,6144]{1,0:T(8,128)S(1)}, f32[16,6144]{1,0:T(8,128)}, u32[]{:S(2)}, u32[]{:S(2)}) collective-permute-start(f32[16,6144]{1,0:T(8,128)S(1)} %get-tuple-element.17), channel_id=1, source_target_pairs={{0,3},{1,4},{2,5},{3,6},{4,7},{5,8},{6,9},{7,10},{8,11},{9,12},{10... | collective-permute-start | bytes 1179656
  404.5 50.3 %collective-permute-start.9 = (f32[16,6144]{1,0:T(8,128)S(1)}, f32[16,6144]{1,0:T(8,128)}, u32[]{:S(2)}, u32[]{:S(2)}) collective-permute-start(f32[16,6144]{1,0:T(8,128)S(1)} %get-tuple-element.17), channel_id=1, source_target_pairs={{0,2},{1,3},{2,4},{3,5},{4,6},{5,7},{6,8},{7,9},{8,10},{9,11},{10,... | collective-permute-start | bytes 1179656
  406.5 49.6 %collective-permute-start.8 = (f32[16,6144]{1,0:T(8,128)S(1)}, f32[16,6144]{1,0:T(8,128)}, u32[]{:S(2)}, u32[]{:S(2)}) collective-permute-start(f32[16,6144]{1,0:T(8,128)S(1)} %get-tuple-element.17), channel_id=1, source_target_pairs={{0,1},{1,2},{2,3},{3,4},{4,5},{5,6},{6,7},{7,8},{8,9},{9,10},{10,1... | collective-permute-start | bytes 1179656
  416.2 68.3 %collective-permute-start.6 = (f32[16,6144]{1,0:T(8,128)S(1)}, f32[16,6144]{1,0:T(8,128)}, u32[]{:S(2)}, u32[]{:S(2)}) collective-permute-start(f32[16,6144]{1,0:T(8,128)S(1)} %get-tuple-element.18), channel_id=1, source_target_pairs={{0,3},{1,4},{2,5},{3,6},{4,7},{5,8},{6,9},{7,10},{8,11},{9,12},{10... | collective-permute-start | bytes 1179656
  422.1 28.8 %collective-permute-start.11 = (f32[12,6144]{1,0:T(8,128)S(1)}, f32[12,6144]{1,0:T(8,128)}, u32[]{:S(2)}, u32[]{:S(2)}) collective-permute-start(f32[12,6144]{1,0:T(8,128)S(1)} %slice.122), channel_id=1, source_target_pairs={{0,4},{1,5},{2,6},{3,7},{4,8},{5,9},{6,10},{7,11},{8,12},{9,13},{1... | collective-permute-start | bytes 884744
  450.9 36.7 %collective-permute-start.5 = (f32[16,6144]{1,0:T(8,128)S(1)}, f32[16,6144]{1,0:T(8,128)S(1)}, u32[]{:S(2)}, u32[]{:S(2)}) collective-permute-start(f32[16,6144]{1,0:T(8,128)S(1)} %get-tuple-element.18), channel_id=1, source_target_pairs={{0,2},{1,3},{2,4},{3,5},{4,6},{5,7},{6,8},{7,9},{8,10},{9,11},{10,... | collective-permute-start | bytes 1179656
  452.7 39.9 %collective-permute-start.4 = (f32[16,6144]{1,0:T(8,128)S(1)}, f32[16,6144]{1,0:T(8,128)}, u32[]{:S(2)}, u32[]{:S(2)}) collective-permute-start(f32[16,6144]{1,0:T(8,128)S(1)} %get-tuple-element.18), channel_id=1, source_target_pairs={{0,1},{1,2},{2,3},{3,4},{4,5},{5,6},{6,7},{7,8},{8,9},{9,10},{10,1... | collective-permute-start | bytes 1179656
  454.8 57.5 %collective-permute-start.2 = (f32[16,6144]{1,0:T(8,128)S(1)}, f32[16,6144]{1,0:T(8,128)S(1)}, u32[]{:S(2)}, u32[]{:S(2)}) collective-permute-start(f32[16,6144]{1,0:T(8,128)S(1)} %get-tuple-element.19), channel_id=1, source_target_pairs={{0,3},{1,4},{2,5},{3,6},{4,7},{5,8},{6,9},{7,10},{8,11},{9,12},{10... | collective-permute-start | bytes 1179656
  456.1 26.7 %collective-permute-start.7 = (f32[12,6144]{1,0:T(8,128)S(1)}, f32[12,6144]{1,0:T(8,128)}, u32[]{:S(2)}, u32[]{:S(2)}) collective-permute-start(f32[12,6144]{1,0:T(8,128)S(1)} %slice.121), channel_id=1, source_target_pairs={{0,4},{1,5},{2,6},{3,7},{4,8},{5,9},{6,10},{7,11},{8,12},{9,13},{1... | collective-permute-start | bytes 884744
  482.7 29.5 %collective-permute-start.1 = (f32[16,6144]{1,0:T(8,128)S(1)}, f32[16,6144]{1,0:T(8,128)S(1)}, u32[]{:S(2)}, u32[]{:S(2)}) collective-permute-start(f32[16,6144]{1,0:T(8,128)S(1)} %get-tuple-element.19), channel_id=1, source_target_pairs={{0,2},{1,3},{2,4},{3,5},{4,6},{5,7},{6,8},{7,9},{8,10},{9,11},{10,... | collective-permute-start | bytes 1179656
  484.5 27.8 %collective-permute-start = (f32[16,6144]{1,0:T(8,128)S(1)}, f32[16,6144]{1,0:T(8,128)}, u32[]{:S(2)}, u32[]{:S(2)}) collective-permute-start(f32[16,6144]{1,0:T(8,128)S(1)} %get-tuple-element.19), channel_id=1, source_target_pairs={{0,1},{1,2},{2,3},{3,4},{4,5},{5,6},{6,7},{7,8},{8,9},{9,10},{10,1... | collective-permute-start | bytes 1179656
  487.6 24.7 %collective-permute-start.3 = (f32[12,6144]{1,0:T(8,128)S(1)}, f32[12,6144]{1,0:T(8,128)}, u32[]{:S(2)}, u32[]{:S(2)}) collective-permute-start(f32[12,6144]{1,0:T(8,128)S(1)} %slice.120), channel_id=1, source_target_pairs={{0,4},{1,5},{2,6},{3,7},{4,8},{5,9},{6,10},{7,11},{8,12},{9,13},{1... | collective-permute-start | bytes 884744
  540.8 46.8 %copy-start.1 = (bf16[6144,8]{0,1:T(8,128)(2,1)S(1)}, bf16[6144,8]{0,1:T(8,128)(2,1)}, u32[]{:S(2)}) copy-start(bf16[6144,8]{0,1:T(8,128)(2,1)} %param.11) | copy-start | bytes 294916
  (6 other events, 41.5 us)
Sparse Core Ops, SparseCore 0:
  539.5 46.1 reduce-scatter.9
